TPU v7x, 32 devices: a whole 2x2x4 slice. The times are simulated.
32 devices in a mesh: group: 2 (over x), wide: 16 (over z, y, core).
Axes of the slice: x: 2, y: 2, z: 4, core: 2. Of those that a mesh axis runs over, the one named last changes fastest.
Arguments:
- basis: bfloat16 [32, 256, 8192], P(('group', 'wide')), parts along dimension 0, may hold values from -0.0625 to 0.0625
- sat_cond: float32 [32, 8192], P(('group', 'wide')), parts along dimension 0, may hold values from 0.1 to 10
- head: float32 [32, 8192], P(('group', 'wide')), parts along dimension 0, may hold values from -2 to 0.5
- storage: float32 [32, 8192], P(('group', 'wide')), parts along dimension 0, may hold values from 0.5 to 4
- counts: int32 [32], P('group'), parts along dimension 0, may hold values from 64 to 256, as said below
- partner: int32 [32], P('group'), parts along dimension 0, may hold values from 0 to 15, as said below
- owner: int32 [32], P('group'), parts along dimension 0, may hold values from 0 to 15, each once
Outputs:
- diag_rows: float32 [32, 256, 256], P(('group', 'wide')), parts along dimension 0
- coupling_rows: float32 [32, 256, 256], P(('group', 'wide')), parts along dimension 0
There are 2 independent parts, one for each index of `group`. A program takes and returns all parts, laid end to end along the dimension named above; each array names one. Nothing has to cross between parts.
Inputs may be any that keep to these rules, and one draw needn't show every extreme that they name: `counts`: some neighbourhood uses all 256 columns and some uses 256 // 4. partner[partner[i]] = i and partner[i] != i. `owner`: each index appears once.
All inputs are finite; a program needn't handle non-finite values.
Results may differ from a plain program's by a relative error of at most 0.0029.
Values may be sent and summed in bfloat16 or wider, within the bound.
A program may use at most 128 MiB of HBM per device.

v0:
```python
import jax
import jax.numpy as jnp
from jax import lax
from jax.sharding import PartitionSpec as P

LAT = 64
SLAB = 2
OV = 2
FACE = 256


def harmonic(first, second):
    return 2.0 * first * second / (first + second)


def flat_image(block_rows, conduct, stored, row_len):
    values = block_rows.astype(jnp.float32)
    result = stored * values
    plane = conduct.shape[1]
    inside = (jnp.arange(plane - 1, dtype=jnp.int32) + 1) % row_len != 0
    trans_x = jnp.where(inside[None, :], harmonic(conduct[:, 1:], conduct[:, :-1]), 0.0)
    flux_x = trans_x * (values[..., 1:] - values[..., :-1])
    result = (
        result
        + jnp.pad(flux_x, ((0, 0), (0, 0), (1, 0)))
        - jnp.pad(flux_x, ((0, 0), (0, 0), (0, 1)))
    )
    trans_y = harmonic(conduct[:, row_len:], conduct[:, :-row_len])
    flux_y = trans_y * (values[..., row_len:] - values[..., :-row_len])
    result = (
        result
        + jnp.pad(flux_y, ((0, 0), (0, 0), (row_len, 0)))
        - jnp.pad(flux_y, ((0, 0), (0, 0), (0, row_len)))
    )
    trans_z = harmonic(conduct[1:, :], conduct[:-1, :])
    flux_z = trans_z * (values[:, 1:, :] - values[:, :-1, :])
    result = (
        result
        + jnp.pad(flux_z, ((0, 0), (1, 0), (0, 0)))
        - jnp.pad(flux_z, ((0, 0), (0, 1), (0, 0)))
    )
    return result.astype(jnp.bfloat16)


def local(basis, sat_cond, head, storage, counts, partner, owner):
    rows_total = basis.shape[1]
    cells_total = basis.shape[2]
    axis_width = lax.axis_size("wide")
    own_index = lax.axis_index("wide")
    slot_iota = jnp.arange(axis_width, dtype=jnp.int32)
    own_count = jnp.sum(jnp.where(slot_iota == own_index, counts, 0))
    own_partner = jnp.sum(jnp.where(slot_iota == own_index, partner, 0))
    row_iota = jnp.arange(rows_total, dtype=jnp.int32)[:, None]
    masked = jnp.where(row_iota < own_count, basis[0], jnp.zeros((), jnp.bfloat16))
    plane = LAT * LAT
    conduct = (sat_cond[0] * jnp.exp(head[0])).reshape(SLAB, plane)
    stored = storage[0].reshape(SLAB, plane)
    west = masked.reshape(rows_total, SLAB, LAT, LAT)[..., :OV].reshape(rows_total, FACE)
    pieces = lax.all_gather(west.reshape(1, rows_total, FACE), "wide", axis=0, tiled=True)
    chosen = jnp.arange(pieces.shape[0], dtype=jnp.int32) == own_partner
    facing = jnp.sum(
        jnp.where(chosen[:, None, None], pieces.astype(jnp.float32), 0.0), axis=0
    ).astype(jnp.bfloat16)

    def image_block(block_rows):
        return flat_image(block_rows, conduct, stored, LAT)

    image = lax.map(image_block, masked.reshape(rows_total // 64, 64, SLAB, plane)).reshape(
        rows_total, cells_total
    )
    diag_block = lax.dot_general(
        masked, image, (((1,), (1,)), ((), ())), preferred_element_type=jnp.float32
    )
    east = image.reshape(rows_total, SLAB, LAT, LAT)[..., LAT - OV :].reshape(rows_total, FACE)
    coupling = lax.dot_general(
        east, facing, (((1,), (1,)), ((), ())), preferred_element_type=jnp.float32
    )
    inverse = jnp.sum(
        jnp.where(owner[None, :] == slot_iota[:, None], slot_iota[None, :], 0), axis=1
    )
    piece_rows = rows_total // axis_width
    diag_spread, coupling_spread = (
        lax.all_to_all(
            diag_block.reshape(axis_width, piece_rows, rows_total),
            "wide",
            split_axis=0,
            concat_axis=0,
            tiled=True,
        ),
        lax.all_to_all(
            coupling.reshape(axis_width, piece_rows, rows_total),
            "wide",
            split_axis=0,
            concat_axis=0,
            tiled=True,
        ),
    )
    diag_routed = jnp.take(diag_spread, inverse, axis=0)
    coupling_routed = jnp.take(coupling_spread, inverse, axis=0)
    diag_owned, coupling_owned = (
        lax.all_to_all(diag_routed, "wide", split_axis=0, concat_axis=0, tiled=True),
        lax.all_to_all(coupling_routed, "wide", split_axis=0, concat_axis=0, tiled=True),
    )
    return (
        diag_owned.reshape(1, rows_total, rows_total),
        coupling_owned.reshape(1, rows_total, rows_total),
    )


def solution(mesh):
    placed = (
        P(("group", "wide"), None, None),
        P(("group", "wide"), None),
        P(("group", "wide"), None),
        P(("group", "wide"), None),
        P("group"),
        P("group"),
        P("group"),
    )
    return jax.shard_map(
        local,
        mesh=mesh,
        in_specs=placed,
        out_specs=(P(("group", "wide"), None, None), P(("group", "wide"), None, None)),
        check_vma=False,
    )
```

profile of v0, /device:TPU:0, one launch (start us, length us, event | category | flops | bytes accessed | tf_op | source)
XLA Modules:
  0.0 226.2 jit_solution(4022413804753216869)
XLA Ops:
  9.0 6.4 %copy.22 = bf16[1,256,8192]{1,2,0:T(8,128)(2,1)} copy(bf16[1,256,8192]{2,1,0:T(8,128)(2,1)} %param.11) | data formatting | bytes 8388608 | tf_op args[0]
  18.0 7.8 %squeeze.12 = bf16[4,64,2,4096]{3,2,1,0:T(2,128)(2,1)} reshape(bf16[1,256,8192]{2,1,0:T(8,128)(2,1)} %param.11) | data formatting | bytes 8388608 | tf_op jit(solution)/shard_map/squeeze | solution.py:54
  27.4 7.8 %broadcast_select_fusion.1 = bf16[4,64,2,4096]{3,2,1,0:T(2,128)(2,1)} fusion(bf16[4,64,2,4096]{3,2,1,0:T(2,128)(2,1)} %squeeze.12, pred[4,64]{1,0:T(4,128)(4,1)S(1)} %add_compare_fusion.1), kind=kLoop, calls=%fused_computation.23 | loop fusion | flops 2097152 | bytes 8388864 | tf_op jit(solution)/shard_map/jit(_where)/select_n | solution.py:54
  35.2 73.0 %while.13 = (s32[]{:T(128)}, bf16[4,64,2,4096]{3,2,1,0:T(2,128)(2,1)}, f32[1,8192]{1,0:T(1,128)S(1)}, bf16[4,64,2,4096]{3,2,1,0:T(2,128)(2,1)}, f32[2,4096]{1,0:...) while((s32[]{:T(128)}, ...), condition=%wide.region_2.3_spmd.clone, body=%wide.region_1.2_spmd.sunk.clone | while | flops 7970157 | bytes 26693692 | solution.py:68
  39.9 3.3 %fusion.27 = f32[64,2,4032]{2,1,0:T(2,128)} fusion(f32[64,2,4096]{2,1,0:T(2,128)S(1)} %bitcast_convert_fusion.3, f32[2,4032]{1,0:T(2,128)S(1)} %multiply_divide_fusion.8), kind=kLoop, calls=%fused_computation.3.clone.1.clone | loop fusion | flops 1032192 | bytes 6225408 | tf_op jit(solution)/shard_map/while/body/eval_jaxpr/mul | solution.py:29
  45.9 7.5 %bitcast_dynamic-update-slice_fusion.3 = bf16[4,64,2,4096]{3,2,1,0:T(2,128)(2,1)} fusion(bf16[4,64,2,4096]{3,2,1,0:T(2,128)(2,1)} %get-tuple-element.184, s32[]{:T(128)} %get-tuple-element.183, f32[64,1,4096]{2,1,0:T(1,128)S(1)} %fusion.26, f32[64,2,4032]{2,1,0:T(2,128)} %fusion.27, f32[64,2,4095]{2,1,0:T(2,128)S(1)} %fusion.29, ...), kind=kLoop, calls=%fused_computation.9.clone.1.clone | loop fusion | flops 4718592 | bytes 7372800 | tf_op jit(solution)/shard_map/while/body/jit(dynamic_update_index_in_dim)/dynamic_update_slice | solution.py:68
  58.1 3.3 %fusion.27 = f32[64,2,4032]{2,1,0:T(2,128)} fusion(f32[64,2,4096]{2,1,0:T(2,128)S(1)} %bitcast_convert_fusion.3, f32[2,4032]{1,0:T(2,128)S(1)} %multiply_divide_fusion.8), kind=kLoop, calls=%fused_computation.3.clone.1.clone | loop fusion | flops 1032192 | bytes 6225408 | tf_op jit(solution)/shard_map/while/body/eval_jaxpr/mul | solution.py:29
  64.2 7.5 %bitcast_dynamic-update-slice_fusion.3 = bf16[4,64,2,4096]{3,2,1,0:T(2,128)(2,1)} fusion(bf16[4,64,2,4096]{3,2,1,0:T(2,128)(2,1)} %get-tuple-element.184, s32[]{:T(128)} %get-tuple-element.183, f32[64,1,4096]{2,1,0:T(1,128)S(1)} %fusion.26, f32[64,2,4032]{2,1,0:T(2,128)} %fusion.27, f32[64,2,4095]{2,1,0:T(2,128)S(1)} %fusion.29, ...), kind=kLoop, calls=%fused_computation.9.clone.1.clone | loop fusion | flops 4718592 | bytes 7372800 | tf_op jit(solution)/shard_map/while/body/jit(dynamic_update_index_in_dim)/dynamic_update_slice | solution.py:68
  76.4 3.3 %fusion.27 = f32[64,2,4032]{2,1,0:T(2,128)} fusion(f32[64,2,4096]{2,1,0:T(2,128)S(1)} %bitcast_convert_fusion.3, f32[2,4032]{1,0:T(2,128)S(1)} %multiply_divide_fusion.8), kind=kLoop, calls=%fused_computation.3.clone.1.clone | loop fusion | flops 1032192 | bytes 6225408 | tf_op jit(solution)/shard_map/while/body/eval_jaxpr/mul | solution.py:29
  82.4 7.5 %bitcast_dynamic-update-slice_fusion.3 = bf16[4,64,2,4096]{3,2,1,0:T(2,128)(2,1)} fusion(bf16[4,64,2,4096]{3,2,1,0:T(2,128)(2,1)} %get-tuple-element.184, s32[]{:T(128)} %get-tuple-element.183, f32[64,1,4096]{2,1,0:T(1,128)S(1)} %fusion.26, f32[64,2,4032]{2,1,0:T(2,128)} %fusion.27, f32[64,2,4095]{2,1,0:T(2,128)S(1)} %fusion.29, ...), kind=kLoop, calls=%fused_computation.9.clone.1.clone | loop fusion | flops 4718592 | bytes 7372800 | tf_op jit(solution)/shard_map/while/body/jit(dynamic_update_index_in_dim)/dynamic_update_slice | solution.py:68
  94.6 3.3 %fusion.27 = f32[64,2,4032]{2,1,0:T(2,128)} fusion(f32[64,2,4096]{2,1,0:T(2,128)S(1)} %bitcast_convert_fusion.3, f32[2,4032]{1,0:T(2,128)S(1)} %multiply_divide_fusion.8), kind=kLoop, calls=%fused_computation.3.clone.1.clone | loop fusion | flops 1032192 | bytes 6225408 | tf_op jit(solution)/shard_map/while/body/eval_jaxpr/mul | solution.py:29
  100.7 7.5 %bitcast_dynamic-update-slice_fusion.3 = bf16[4,64,2,4096]{3,2,1,0:T(2,128)(2,1)} fusion(bf16[4,64,2,4096]{3,2,1,0:T(2,128)(2,1)} %get-tuple-element.184, s32[]{:T(128)} %get-tuple-element.183, f32[64,1,4096]{2,1,0:T(1,128)S(1)} %fusion.26, f32[64,2,4032]{2,1,0:T(2,128)} %fusion.27, f32[64,2,4095]{2,1,0:T(2,128)S(1)} %fusion.29, ...), kind=kLoop, calls=%fused_computation.9.clone.1.clone | loop fusion | flops 4718592 | bytes 7372800 | tf_op jit(solution)/shard_map/while/body/jit(dynamic_update_index_in_dim)/dynamic_update_slice | solution.py:68
  108.2 7.8 %reshape.127 = bf16[256,8192,1]{1,0,2:T(8,128)(2,1)} reshape(bf16[4,64,2,4096]{3,2,1,0:T(2,128)(2,1)} %get-tuple-element.86) | data formatting | bytes 8388608 | tf_op jit(solution)/shard_map/reshape | solution.py:68
  116.7 2.7 %broadcast_select_fusion.2 = bf16[1,256,8192]{2,1,0:T(8,128)(2,1)S(1)} fusion(bf16[1,256,8192]{2,1,0:T(8,128)(2,1)} %param.11, pred[256]{0:T(512)(128)(4,1)S(1)} %lt.41), kind=kLoop, calls=%fused_computation.25 | loop fusion | flops 2097152 | bytes 8388864 | tf_op jit(solution)/shard_map/jit(_where)/select_n | solution.py:54
  122.1 7.3 %all-to-all-start = ((f32[16,16,256]{2,1,0:T(8,128)}), f32[16,16,256]{2,1,0:T(8,128)S(1)}, u32[]{:S(2)}, u32[]{:S(2)}) async-start(f32[16,16,256]{2,1,0:T(8,128)} %fusion.15), calls=%async_computation | async-start | bytes 524288 | tf_op jit(solution)/shard_map/all_to_all | solution.py:83
  129.5 7.1 %copy.20 = bf16[4,64,2,4096]{3,1,0,2:T(8,128)(2,1)} copy(bf16[4,64,2,4096]{3,2,1,0:T(2,128)(2,1)} %get-tuple-element.86) | data formatting | bytes 8388608 | tf_op jit(solution)/shard_map/while | solution.py:68
  136.5 12.6 %reshape_reshape.6 = bf16[256,2,64,64]{3,2,0,1:T(8,128)(2,1)} reshape(bf16[4,64,2,4096]{3,1,0,2:T(8,128)(2,1)} %copy.20) | data formatting | bytes 8388608 | tf_op jit(solution)/shard_map/reshape;reshape | solution.py:74
  149.1 9.2 %slice.122 = bf16[256,2,64,2]{3,2,0,1:T(8,128)(2,1)} slice(bf16[256,2,64,64]{3,2,0,1:T(8,128)(2,1)} %reshape_reshape.6), slice={[0:256], [0:2], [0:64], [62:64]} | slice | bytes 262144 | tf_op jit(solution)/shard_map/slice | solution.py:74
  158.4 10.4 %copy.21 = bf16[256,2,64,2]{0,3,2,1:T(2,128)(2,1)S(1)} copy(bf16[256,2,64,2]{3,2,0,1:T(8,128)(2,1)} %slice.122) | data formatting | bytes 262144 | tf_op jit(solution)/shard_map/slice | solution.py:74
  174.1 6.0 %all-to-all-start.2 = ((f32[16,16,256]{2,1,0:T(8,128)}), f32[16,16,256]{2,1,0:T(8,128)S(1)}, u32[]{:S(2)}, u32[]{:S(2)}) async-start(f32[16,16,256]{2,1,0:T(8,128)} %fusion.8), calls=%async_computation.2 | async-start | bytes 524288 | tf_op jit(solution)/shard_map/all_to_all | solution.py:90
  180.7 9.4 %all-to-all-done.2 = f32[16,16,256]{2,1,0:T(8,128)S(1)} async-done(((f32[16,16,256]{2,1,0:T(8,128)}), f32[16,16,256]{2,1,0:T(8,128)S(1)}, u32[]{:S(2)}, u32[]{:S(2)}) %all-to-all-start.2) | async-done | bytes 262176 | tf_op jit(solution)/shard_map/all_to_all | solution.py:90
  191.5 12.8 %all_to_all.20 = f32[16,16,256]{2,1,0:T(8,128)S(1)} all-to-all(f32[16,16,256]{2,1,0:T(8,128)S(1)} %get-tuple-element.106), channel_id=1, replica_groups=mesh['group'=2,'wide'=16] {'wide'}, dimensions={0} | all-to-all | bytes 524288 | tf_op jit(solution)/shard_map/all_to_all | solution.py:101
  204.4 3.5 %all-to-all-start.3 = ((f32[16,16,256]{2,1,0:T(8,128)}), f32[16,16,256]{2,1,0:T(8,128)S(1)}, u32[]{:S(2)}, u32[]{:S(2)}) async-start(f32[16,16,256]{2,1,0:T(8,128)} %get-tuple-element.105), calls=%async_computation.3 | async-start | bytes 524288 | tf_op jit(solution)/shard_map/all_to_all | solution.py:102
  207.9 10.0 %all-to-all-done.3 = f32[16,16,256]{2,1,0:T(8,128)S(1)} async-done(((f32[16,16,256]{2,1,0:T(8,128)}), f32[16,16,256]{2,1,0:T(8,128)S(1)}, u32[]{:S(2)}, u32[]{:S(2)}) %all-to-all-start.3) | async-done | bytes 262176 | tf_op jit(solution)/shard_map/all_to_all | solution.py:102
  (87 shorter events, 47.5 us)
Async XLA Ops:
  7.2 163.6 %all-gather.2.cloned.1.call-start = ((), (), s32[]{:S(2)}) async-start(), calls=%async_computation.4 | async-start | bytes 2228224 | tf_op jit(solution)/shard_map/all_gather | solution.py:59
  18.0 8.4 %copy-start.2 = (f32[1,8192]{1,0:T(1,128)S(1)}, f32[1,8192]{1,0:T(1,128)}, u32[]{:S(2)}) copy-start(f32[1,8192]{1,0:T(1,128)} %param.12) | copy-start | bytes 98308
  18.0 8.3 %copy-start.3 = (f32[1,8192]{1,0:T(1,128)S(1)}, f32[1,8192]{1,0:T(1,128)}, u32[]{:S(2)}) copy-start(f32[1,8192]{1,0:T(1,128)} %param.13) | copy-start | bytes 98308
  27.4 7.8 %copy-start.1 = (f32[1,8192]{1,0:T(1,128)S(1)}, f32[1,8192]{1,0:T(1,128)}, u32[]{:S(2)}) copy-start(f32[1,8192]{1,0:T(1,128)} %param.14) | copy-start | bytes 98308
  116.7 3.5 %copy-start = (bf16[256,8192,1]{1,0,2:T(8,128)(2,1)S(1)}, bf16[256,8192,1]{1,0,2:T(8,128)(2,1)}, u32[]{:S(2)}) copy-start(bf16[256,8192,1]{1,0,2:T(8,128)(2,1)} %reshape.127) | copy-start | bytes 12582916
  122.1 52.0 %all-to-all-start = ((f32[16,16,256]{2,1,0:T(8,128)}), f32[16,16,256]{2,1,0:T(8,128)S(1)}, u32[]{:S(2)}, u32[]{:S(2)}) async-start(f32[16,16,256]{2,1,0:T(8,128)} %fusion.15), calls=%async_computation | async-start | bytes 524288 | tf_op jit(solution)/shard_map/all_to_all | solution.py:83
  158.4 11.1 %copy-start.4 = (s32[16]{0:T(128)S(1)}, s32[16]{0:T(128)}, u32[]{:S(2)}) copy-start(s32[16]{0:T(128)} %param.16) | copy-start | bytes 196
  158.4 12.3 %copy-start.5 = (s32[16]{0:T(128)S(1)}, s32[16]{0:T(128)}, u32[]{:S(2)}) copy-start(s32[16]{0:T(128)} %param.17) | copy-start | bytes 196
  174.1 16.1 %all-to-all-start.2 = ((f32[16,16,256]{2,1,0:T(8,128)}), f32[16,16,256]{2,1,0:T(8,128)S(1)}, u32[]{:S(2)}, u32[]{:S(2)}) async-start(f32[16,16,256]{2,1,0:T(8,128)} %fusion.8), calls=%async_computation.2 | async-start | bytes 524288 | tf_op jit(solution)/shard_map/all_to_all | solution.py:90
  204.4 13.5 %all-to-all-start.3 = ((f32[16,16,256]{2,1,0:T(8,128)}), f32[16,16,256]{2,1,0:T(8,128)S(1)}, u32[]{:S(2)}, u32[]{:S(2)}) async-start(f32[16,16,256]{2,1,0:T(8,128)} %get-tuple-element.105), calls=%async_computation.3 | async-start | bytes 524288 | tf_op jit(solution)/shard_map/all_to_all | solution.py:102
Sparse Core Ops, SparseCore 0:
  17.5 44.0 all-gather.1
where the time goes:
time: 228 us; the launch traced here: 226 us
  other arithmetic  90.2 us (40%)
  local copies, waits for them, and re-layouts  69.2 us (30%)
  waiting for transfers between devices  19.5 us (9%)
  starting transfers between devices  16.9 us (7%)
  between operations  14.3 us (6%)
  blocking collectives  12.8 us (6%)
  matrix products  3.12 us (1%)
    dynamic_update_slice x4, other arithmetic, local(): lax.map(image_block, masked.reshape(rows_total // 64, 64, SLAB, plane))  30.1 us
    slice x2, local copies, waits for them, and re-layouts, local(): image.reshape(rows_total, SLAB, LAT, LAT)[..., LAT - OV:]  19.6 us
    mul x4, other arithmetic, flat_image(): flux_y = trans_y * (values[..., row_len:] - values[..., :-row_len])  13.2 us
    all_to_all x1, blocking collectives, local(): lax.all_to_all(diag_routed, 'wide', split_axis=0, concat_axis=0, tiled=True)  12.8 us
    another operation x1, local copies, waits for them, and re-layouts, local(): image.reshape(rows_total, SLAB, LAT, LAT)[..., LAT - OV:]  12.6 us
    select_n x3, other arithmetic, local(): jnp.where(row_iota < own_count, basis[0], jnp.zeros((), jnp.bfloat16))  11.6 us
    all_to_all x1, waiting for transfers between devices, local(): lax.all_to_all(coupling_routed, 'wide', split_axis=0, concat_axis=0, tile...  10 us
    all_to_all x1, waiting for transfers between devices, local(): lax.all_to_all(coupling.reshape(axis_width, piece_rows, rows_total), 'wid...  9.43 us
  transfers between devices with their start and end apart: 4, of which 2 were waited for; matrix products, arithmetic and copies ran while one was open for 66% of the time, Pallas kernels for 0%

commit v1 on v0

v1 whole, which is shorter than its diff:
```python
import functools

import jax
import jax.numpy as jnp
from jax import lax
from jax.experimental import pallas as pl
from jax.experimental.pallas import tpu as pltpu
from jax.sharding import PartitionSpec as P

LAT = 64
SLAB = 2
FACE = 256
LANES = 128
ROWS = 16
TILES = LAT * LAT // LANES
GROUP = 16
HALVES = 2


def harmonic(first, second):
    return 2.0 * first * second / (first + second)


def tile_of(plane, tile):
    start = plane * LAT * LAT + tile * LANES
    return slice(start, start + LANES)


def coefficients(sat_ref, head_ref, storage_ref, coef_ref):
    lane = lax.broadcasted_iota(jnp.int32, (8, LANES), 1)
    low = lane < LAT
    inside = lane % LAT != LAT - 1

    def wide(ref, plane, tile):
        return jnp.broadcast_to(ref[0:1, tile_of(plane, tile)], (8, LANES))

    conduct = [
        [wide(sat_ref, z, j) * jnp.exp(wide(head_ref, z, j)) for j in range(TILES)]
        for z in range(SLAB)
    ]
    for j in range(TILES):
        along_z = harmonic(conduct[0][j], conduct[1][j])
        for z in range(SLAB):
            own = conduct[z][j]
            right = jnp.where(inside, harmonic(own, pltpu.roll(own, LANES - 1, 1)), 0.0)
            left = pltpu.roll(right, 1, 1)
            within = harmonic(own, pltpu.roll(own, LAT, 1))
            before = pltpu.roll(conduct[z][max(j - 1, 0)], LAT, 1)
            after = pltpu.roll(conduct[z][min(j + 1, TILES - 1)], LAT, 1)
            across = harmonic(own, jnp.where(low, before, after))
            if j == 0:
                across = jnp.where(low, 0.0, across)
            if j == TILES - 1:
                across = jnp.where(low, across, 0.0)
            total = wide(storage_ref, z, j) + right + left + within + across + along_z
            for n, value in enumerate((total, right, left, within, across, along_z)):
                coef_ref[n, :, tile_of(z, j)] = value


def kernel(
    width,
    piece_rows,
    basis_ref,
    sat_ref,
    head_ref,
    storage_ref,
    counts_ref,
    partner_ref,
    owner_ref,
    diag_ref,
    coupling_ref,
    basis_v,
    image_v,
    coef_ref,
    face_src,
    face_recv,
    face_stage,
    face_fin,
    diag_src,
    diag_recv_0,
    diag_recv_1,
    diag_stage,
    diag_fin,
    inverse_ref,
    load_sem,
    face_sems,
    diag_sems,
):
    diag_recv = (diag_recv_0, diag_recv_1)
    rows_total = basis_v.shape[0]
    pieces = rows_total // piece_rows
    stride = width // pieces
    half_rows = rows_total // HALVES
    me = lax.axis_index("wide")
    own_piece = me // stride
    is_middle = lax.rem(me, stride) == 0

    loads = []
    for h in range(HALVES):
        part = pl.ds(h * half_rows, half_rows)
        loads.append(
            pltpu.make_async_copy(basis_ref.at[0, part], basis_v.at[part], load_sem.at[h])
        )
        loads[-1].start()

    barrier = pltpu.get_barrier_semaphore()

    @pl.loop(1, width)
    def _(step):
        pl.semaphore_signal(
            barrier,
            inc=1,
            device_id={"wide": lax.rem(me + step, width)},
            device_id_type=pl.DeviceIdType.MESH,
        )

    coefficients(sat_ref, head_ref, storage_ref, coef_ref)

    @pl.loop(0, width)
    def _(d):
        found = jnp.int32(0)
        for i in range(width):
            found = jnp.where(owner_ref[i] == d, i, found)
        inverse_ref[d] = found

    pl.semaphore_wait(barrier, width - 1)

    own_count = counts_ref[me]
    lane = lax.broadcasted_iota(jnp.int32, (ROWS, LANES), 1)
    low = lane < LAT
    westerly = lane % LAT < 2

    def copy_to(src, dst, send_sem, recv_sem, target):
        return pltpu.make_async_remote_copy(
            src_ref=src,
            dst_ref=dst,
            send_sem=send_sem,
            recv_sem=recv_sem,
            device_id={"wide": target},
            device_id_type=pl.DeviceIdType.MESH,
        )

    def first_leg(src, recv, sems, piece):
        target = piece * stride
        return copy_to(
            src.at[piece], recv.at[me], sems.at[0, piece], sems.at[1, me], target
        )

    def second_leg(stage, fin, sems, target):
        return copy_to(
            stage.at[target],
            fin.at[own_piece],
            sems.at[2, target],
            sems.at[3, own_piece],
            target,
        )

    groups_per_piece = piece_rows // ROWS

    def image_group(half, step):
        groups = half_rows // ROWS
        local_group = lax.rem(step + me * groups_per_piece, groups)
        row = pl.multiple_of(half * half_rows + local_group * ROWS, ROWS)
        keep = row + lax.broadcasted_iota(jnp.int32, (ROWS, LANES), 0) < own_count
        values = {}
        turned = {}

        def value(z, j):
            if (z, j) not in values:
                values[z, j] = basis_v[pl.ds(row, ROWS), tile_of(z, j)].astype(jnp.float32)
            return values[z, j]

        def turn(z, j):
            j = min(max(j, 0), TILES - 1)
            if (z, j) not in turned:
                turned[z, j] = pltpu.roll(value(z, j), LAT, 1)
            return turned[z, j]

        def coef(n, z, j):
            one = coef_ref[n, :, tile_of(z, j)]
            return jnp.concatenate([one] * (ROWS // 8), axis=0)

        faces = [[None] * (TILES // GROUP) for _ in range(SLAB)]
        for j in range(TILES):
            along_z = coef(5, 0, j)
            shift = 4 * (j % GROUP)
            landing = (lane - (LAT - 2) - shift + LANES) % LAT < 4
            for z in range(SLAB):
                own = value(z, j)
                image = coef(0, z, j) * own
                image = image - coef(1, z, j) * pltpu.roll(own, LANES - 1, 1)
                image = image - coef(2, z, j) * pltpu.roll(own, 1, 1)
                image = image - coef(3, z, j) * turn(z, j)
                image = image - coef(4, z, j) * jnp.where(low, turn(z, j - 1), turn(z, j + 1))
                image = image - along_z * value(1 - z, j)
                image_v[pl.ds(pl.multiple_of(local_group * ROWS, ROWS), ROWS), tile_of(z, j)] = (
                    image.astype(jnp.bfloat16)
                )
                mixed = jnp.where(westerly, own, image)
                if shift:
                    mixed = pltpu.roll(mixed, shift, 1)
                held = faces[z][j // GROUP]
                faces[z][j // GROUP] = mixed if held is None else jnp.where(landing, mixed, held)
        piece = row // piece_rows
        place = pl.multiple_of(lax.rem(row, piece_rows), ROWS)
        flat = [tile for plane in faces for tile in plane]
        for n, tile in enumerate(flat):
            face_src[piece, pl.ds(place, ROWS), n * LANES : (n + 1) * LANES] = jnp.where(
                keep, tile, 0.0
            ).astype(jnp.bfloat16)
        return piece

    def image_half(half):
        piece_per_half = pieces // HALVES

        @pl.loop(0, piece_per_half)
        def _(step):
            piece = None
            for part in range(groups_per_piece):
                piece = image_group(half, step * groups_per_piece + part)

            @pl.when(piece * stride != me)
            def _():
                first_leg(face_src, face_recv, face_sems, piece).start()

            @pl.when(piece * stride == me)
            def _():
                face_recv[me] = face_src[piece]

    def diag_half(half):
        block = lax.dot_general(
            basis_v[...], image_v[...], (((1,), (1,)), ((), ())), preferred_element_type=jnp.float32
        )
        row = lax.broadcasted_iota(jnp.int32, block.shape, 0)
        column = lax.broadcasted_iota(jnp.int32, block.shape, 1) + half * half_rows
        block = jnp.where((row < own_count) & (column < own_count), block, 0.0)
        diag_src[half] = block.astype(jnp.bfloat16).reshape(pieces, piece_rows, half_rows)

        @pl.loop(0, pieces)
        def _(step):
            piece = lax.rem(step + own_piece, pieces)

            @pl.when(piece * stride != me)
            def _():
                first_leg(diag_src.at[half], diag_recv[half], diag_sems.at[half], piece).start()

            @pl.when(piece * stride == me)
            def _():
                diag_recv[half][me] = diag_src[half, piece]

    def wait_first(src, recv, sems):
        @pl.loop(0, width)
        def _(source):
            @pl.when(source != me)
            def _():
                copy_to(
                    src.at[own_piece], recv.at[source], sems.at[0, own_piece], sems.at[1, source], source
                ).wait_recv()

    def wait_second(stage, fin, sems):
        @pl.loop(0, pieces)
        def _(piece):
            @pl.when(piece * stride != me)
            def _():
                copy_to(
                    stage.at[me], fin.at[piece], sems.at[2, me], sems.at[3, piece], piece * stride
                ).wait_recv()

    def forward(pick, src, recv, stage, fin, sems):
        @pl.when(is_middle)
        def _():
            wait_first(src, recv, sems)

            @pl.loop(1, width + 1)
            def _(step):
                target = lax.rem(me + step, width)
                taken = pick(inverse_ref[target])

                @pl.when(target != me)
                def _():
                    stage[target] = taken
                    second_leg(stage, fin, sems, target).start()

                @pl.when(target == me)
                def _():
                    fin[own_piece] = taken

    def wait_sent(src, recv, stage, fin, sems):
        @pl.loop(0, pieces)
        def _(piece):
            @pl.when(piece * stride != me)
            def _():
                first_leg(src, recv, sems, piece).wait_send()

        @pl.when(is_middle)
        def _():
            @pl.loop(0, width)
            def _(target):
                @pl.when(target != me)
                def _():
                    second_leg(stage, fin, sems, target).wait_send()

    face_lane = lax.broadcasted_iota(jnp.int32, (piece_rows, 2 * FACE), 1)
    easterly = face_lane % 4 >= 2

    def pick_face(source):
        east = face_recv[source].astype(jnp.float32)
        west = face_recv[partner_ref[source]].astype(jnp.float32)
        return jnp.where(easterly, east, west).astype(jnp.bfloat16)

    loads[0].wait()
    image_half(0)
    loads[1].wait()
    diag_half(0)
    image_half(1)
    diag_half(1)
    face_refs = (face_src, face_recv, face_stage, face_fin, face_sems)
    diag_refs = [
        (diag_src.at[h], diag_recv[h], diag_stage.at[h], diag_fin.at[h], diag_sems.at[h])
        for h in range(HALVES)
    ]
    forward(pick_face, *face_refs)
    for h in range(HALVES):
        forward(lambda source, h=h: diag_recv[h][source], *diag_refs[h])

    wait_second(face_stage, face_fin, face_sems)
    both = face_fin[...].reshape(rows_total, 2 * FACE).astype(jnp.float32)
    easts, wests = [], []
    east_lane = lax.broadcasted_iota(jnp.int32, (rows_total, LANES), 1) % 4 >= 2
    for n in range(2 * FACE // LANES):
        tile = both[:, n * LANES : (n + 1) * LANES]
        easts.append(jnp.where(east_lane, tile, 0.0).astype(jnp.bfloat16))
        wests.append(pltpu.roll(tile, LAT - 2, 1).astype(jnp.bfloat16))
    coupling_ref[0] = lax.dot_general(
        jnp.concatenate(easts, axis=1),
        jnp.concatenate(wests, axis=1),
        (((1,), (1,)), ((), ())),
        preferred_element_type=jnp.float32,
    )
    for h in range(HALVES):
        wait_second(diag_stage.at[h], diag_fin.at[h], diag_sems.at[h])
        diag_ref[0, :, h * half_rows : (h + 1) * half_rows] = (
            diag_fin[h].reshape(rows_total, half_rows).astype(jnp.float32)
        )
    wait_sent(*face_refs)
    for h in range(HALVES):
        wait_sent(*diag_refs[h])


def local(width, basis, sat_cond, head, storage, counts, partner, owner):
    rows = basis.shape[1]
    cells = basis.shape[2]
    piece_rows = max(ROWS, rows // width)
    pieces = rows // piece_rows
    half = rows // HALVES
    bf16 = jnp.bfloat16
    out = jax.ShapeDtypeStruct((1, rows, rows), jnp.float32)
    vmem = pl.BlockSpec(memory_space=pltpu.VMEM)
    smem = pl.BlockSpec(memory_space=pltpu.SMEM)
    return pl.pallas_call(
        functools.partial(kernel, width, piece_rows),
        out_shape=(out, out),
        in_specs=[pl.BlockSpec(memory_space=pl.ANY), vmem, vmem, vmem, smem, smem, smem],
        out_specs=(vmem, vmem),
        scratch_shapes=[
            pltpu.VMEM((rows, cells), bf16),
            pltpu.VMEM((half, cells), bf16),
            pltpu.VMEM((6, 8, cells), jnp.float32),
            pltpu.VMEM((pieces, piece_rows, 2 * FACE), bf16),
            pltpu.VMEM((width, piece_rows, 2 * FACE), bf16),
            pltpu.VMEM((width, piece_rows, 2 * FACE), bf16),
            pltpu.VMEM((pieces, piece_rows, 2 * FACE), bf16),
            pltpu.VMEM((HALVES, pieces, piece_rows, half), bf16),
            pltpu.VMEM((width, piece_rows, half), bf16),
            pltpu.VMEM((width, piece_rows, half), bf16),
            pltpu.VMEM((HALVES, width, piece_rows, half), bf16),
            pltpu.VMEM((HALVES, pieces, piece_rows, half), bf16),
            pltpu.SMEM((width,), jnp.int32),
            pltpu.SemaphoreType.DMA((HALVES,)),
            pltpu.SemaphoreType.DMA((4, width)),
            pltpu.SemaphoreType.DMA((HALVES, 4, width)),
        ],
        compiler_params=pltpu.CompilerParams(
            collective_id=0, has_side_effects=True, vmem_limit_bytes=40 * 1024 * 1024
        ),
    )(basis, sat_cond, head, storage, counts, partner, owner)


def solution(mesh):
    placed = (
        P(("group", "wide"), None, None),
        P(("group", "wide"), None),
        P(("group", "wide"), None),
        P(("group", "wide"), None),
        P("group"),
        P("group"),
        P("group"),
    )
    return jax.shard_map(
        functools.partial(local, mesh.shape["wide"]),
        mesh=mesh,
        in_specs=placed,
        out_specs=(P(("group", "wide"), None, None), P(("group", "wide"), None, None)),
        check_vma=False,
    )
```

time: 228 us -> 79.6 us (0.35)
  other arithmetic: 90.2 us -> 0 us
  Pallas kernels: 0 us -> 70.8 us
  local copies, waits for them, and re-layouts: 69.2 us -> 7.82 us
  waiting for transfers between devices: 19.5 us -> 0 us
  starting transfers between devices: 16.9 us -> 0 us
  between operations: 14.3 us -> 0.66 us
  blocking collectives: 12.8 us -> 0 us
  matrix products: 3.12 us -> 0 us
    pallas_call x0 -> x1, Pallas kernels: none -> 70.8 us  [local(): pl.pallas_call(functools.partial(kernel, width, piece_rows), out_shape=(o...]
    dynamic_update_slice x4 -> x0, other arithmetic: 30.1 us -> none  [local(): lax.map(image_block, masked.reshape(rows_total // 64, 64, SLAB, plane))]
    mul x13 -> x0, other arithmetic: 28.8 us -> none  [the longest x4 13.2 us: flat_image(): flux_y = trans_y * (values[..., row_len:] - values[..., :-row_len])]
    slice x2 -> x0, local copies, waits for them, and re-layouts: 19.6 us -> none  [local(): image.reshape(rows_total, SLAB, LAT, LAT)[..., LAT - OV:]]
    all_to_all x3 -> x0, waiting for transfers between devices: 19.4 us -> none  [the longest x1 10 us: local(): lax.all_to_all(coupling_routed, 'wide', split_axis=0, concat_axis=0, tile...]
    all_to_all x3 -> x0, starting transfers between devices: 16.9 us -> none  [the longest x1 7.32 us: local(): lax.all_to_all(diag_block.reshape(axis_width, piece_rows, rows_total), 'w...]
    another operation x7 -> x0, local copies, waits for them, and re-layouts: 15.7 us -> none  [the longest x1 12.6 us: local(): image.reshape(rows_total, SLAB, LAT, LAT)[..., LAT - OV:]]
    select_n x9 -> x0, other arithmetic: 12.9 us -> none  [the longest x3 11.6 us: local(): jnp.where(row_iota < own_count, basis[0], jnp.zeros((), jnp.bfloat16))]
  transfers between devices with their start and end apart: 4 -> 0, of which waited for: 2 -> 0; matrix products, arithmetic and copies ran while one was open for 66% -> 0% of each run, Pallas kernels for 0% -> 0%
where the time goes in v1:
time: 79.6 us; the launch traced here: 79.2 us
  Pallas kernels  70.8 us (89%)
  local copies, waits for them, and re-layouts  7.82 us (10%)
    pallas_call x1, Pallas kernels, local(): pl.pallas_call(functools.partial(kernel, width, piece_rows), out_shape=(o...  70.8 us
    unnamed x16, local copies, waits for them, and re-layouts  7.82 us

profile of v1, /device:TPU:0, one launch (start us, length us, event | category | flops | bytes accessed | tf_op | source)
XLA Modules:
  0.0 79.2 jit_solution(604580034180282009)
XLA Ops:
  0.6 0.0 copy-start
  0.6 2.2 %copy-done = bf16[1,256,8192]{2,1,0:T(8,128)(2,1)S(1)} copy-done((bf16[1,256,8192]{2,1,0:T(8,128)(2,1)S(1)}, bf16[1,256,8192]{2,1,0:T(8,128)(2,1)}, u32[]{:S(2)}) %copy-start) | copy-done | bytes 4194328
  2.8 0.0 copy-start.1
  2.8 0.8 copy-done.1
  3.6 0.0 copy-start.2
  3.6 0.8 copy-done.2
  4.3 0.0 copy-start.3
  4.3 0.8 copy-done.3
  5.1 0.0 copy-start.4
  5.1 0.7 copy-done.4
  5.8 0.0 copy-start.5
  5.8 0.7 copy-done.5
  6.4 0.0 copy-start.6
  6.4 0.7 copy-done.6
  7.1 70.8 %shard_map.86 = (f32[1,256,256]{2,1,0:T(8,128)S(1)}, f32[1,256,256]{2,1,0:T(8,128)S(1)}) custom-call(bf16[1,256,8192]{2,1,0:T(8,128)(2,1)S(1)} %copy-done, f32[1,8192]{1,0:T(1,128)S(1)} %copy-done.1, f32[1,8192]{1,0:T(1,128)S(1)} %copy-done.2, f32[1,8192]{1,0:T(1,128)S(1)} %copy-done.3, s32[16]{0:T(128)S(1)} %copy-done.4, s32[16]{0:T(128)S(1)} %copy-done.5, ...), custom_call_target="tpu_custom_call" | custom-call | tf_op jit(solution)/shard_map/pallas_call | solution.py:360
  77.8 0.7 copy.11
  78.5 0.7 copy.12
Async XLA Ops:
  0.6 2.2 %copy-start = (bf16[1,256,8192]{2,1,0:T(8,128)(2,1)S(1)}, bf16[1,256,8192]{2,1,0:T(8,128)(2,1)}, u32[]{:S(2)}) copy-start(bf16[1,256,8192]{2,1,0:T(8,128)(2,1)} %basis_ref.1) | copy-start | bytes 12582916
  2.8 0.8 copy-start.1
  3.6 0.8 copy-start.2
  4.3 0.8 copy-start.3
  5.1 0.7 copy-start.4
  5.8 0.7 copy-start.5
  6.4 0.7 copy-start.6

commit v2 on v1

--- a/solution.py
+++ b/solution.py
@@ -157,11 +157,13 @@
 
     groups_per_piece = piece_rows // ROWS
 
+    def group_rows(half, step):
+        local_group = lax.rem(step + me * groups_per_piece, half_rows // ROWS)
+        place = pl.multiple_of(local_group * ROWS, ROWS)
+        return place, pl.multiple_of(half * half_rows + place, ROWS)
+
     def image_group(half, step):
-        groups = half_rows // ROWS
-        local_group = lax.rem(step + me * groups_per_piece, groups)
-        row = pl.multiple_of(half * half_rows + local_group * ROWS, ROWS)
-        keep = row + lax.broadcasted_iota(jnp.int32, (ROWS, LANES), 0) < own_count
+        place, row = group_rows(half, step)
         values = {}
         turned = {}
 
@@ -180,11 +182,8 @@
             one = coef_ref[n, :, tile_of(z, j)]
             return jnp.concatenate([one] * (ROWS // 8), axis=0)
 
-        faces = [[None] * (TILES // GROUP) for _ in range(SLAB)]
         for j in range(TILES):
             along_z = coef(5, 0, j)
-            shift = 4 * (j % GROUP)
-            landing = (lane - (LAT - 2) - shift + LANES) % LAT < 4
             for z in range(SLAB):
                 own = value(z, j)
                 image = coef(0, z, j) * own
@@ -193,31 +192,45 @@
                 image = image - coef(3, z, j) * turn(z, j)
                 image = image - coef(4, z, j) * jnp.where(low, turn(z, j - 1), turn(z, j + 1))
                 image = image - along_z * value(1 - z, j)
-                image_v[pl.ds(pl.multiple_of(local_group * ROWS, ROWS), ROWS), tile_of(z, j)] = (
-                    image.astype(jnp.bfloat16)
-                )
-                mixed = jnp.where(westerly, own, image)
-                if shift:
-                    mixed = pltpu.roll(mixed, shift, 1)
-                held = faces[z][j // GROUP]
-                faces[z][j // GROUP] = mixed if held is None else jnp.where(landing, mixed, held)
+                image_v[pl.ds(place, ROWS), tile_of(z, j)] = image.astype(jnp.bfloat16)
+
+    def face_group(half, step):
+        place, row = group_rows(half, step)
+        keep = row + lax.broadcasted_iota(jnp.int32, (ROWS, LANES), 0) < own_count
         piece = row // piece_rows
-        place = pl.multiple_of(lax.rem(row, piece_rows), ROWS)
-        flat = [tile for plane in faces for tile in plane]
-        for n, tile in enumerate(flat):
-            face_src[piece, pl.ds(place, ROWS), n * LANES : (n + 1) * LANES] = jnp.where(
-                keep, tile, 0.0
-            ).astype(jnp.bfloat16)
+        inner = pl.multiple_of(lax.rem(row, piece_rows), ROWS)
+        for z in range(SLAB):
+            for first in range(0, TILES, GROUP):
+                held = None
+                for j in range(first, first + GROUP):
+                    shift = 4 * (j % GROUP)
+                    landing = (lane - (LAT - 2) - shift + LANES) % LAT < 4
+                    mixed = jnp.where(
+                        westerly,
+                        basis_v[pl.ds(row, ROWS), tile_of(z, j)].astype(jnp.float32),
+                        image_v[pl.ds(place, ROWS), tile_of(z, j)].astype(jnp.float32),
+                    )
+                    if shift:
+                        mixed = pltpu.roll(mixed, shift, 1)
+                    held = mixed if held is None else jnp.where(landing, mixed, held)
+                n = (z * TILES + first) // GROUP
+                face_src[piece, pl.ds(inner, ROWS), n * LANES : (n + 1) * LANES] = jnp.where(
+                    keep, held, 0.0
+                ).astype(jnp.bfloat16)
         return piece
 
     def image_half(half):
         piece_per_half = pieces // HALVES
+
+        @pl.loop(0, half_rows // ROWS)
+        def _(step):
+            image_group(half, step)
 
         @pl.loop(0, piece_per_half)
         def _(step):
             piece = None
             for part in range(groups_per_piece):
-                piece = image_group(half, step * groups_per_piece + part)
+                piece = face_group(half, step * groups_per_piece + part)
 
             @pl.when(piece * stride != me)
             def _():
@@ -381,7 +394,7 @@
             pltpu.SemaphoreType.DMA((HALVES, 4, width)),
         ],
         compiler_params=pltpu.CompilerParams(
-            collective_id=0, has_side_effects=True, vmem_limit_bytes=40 * 1024 * 1024
+            collective_id=0, has_side_effects=True, vmem_limit_bytes=60 * 1024 * 1024
         ),
     )(basis, sat_cond, head, storage, counts, partner, owner)
 

time: 79.6 us -> 42.5 us (0.53)
  Pallas kernels: 70.8 us -> 38.2 us
  local copies, waits for them, and re-layouts: 7.82 us -> 3.34 us
    pallas_call x1, Pallas kernels: 70.8 us -> 38.2 us  [local(): pl.pallas_call(functools.partial(kernel, width, piece_rows), out_shape=(o...]
    unnamed x16 -> x2, local copies, waits for them, and re-layouts: 7.82 us -> 3.34 us
where the time goes in v2:
time: 42.5 us; the launch traced here: 42.2 us
  Pallas kernels  38.2 us (90%)
  local copies, waits for them, and re-layouts  3.34 us (8%)
  between operations  0.64 us (2%)
    pallas_call x1, Pallas kernels, local(): pl.pallas_call(functools.partial(kernel, width, piece_rows), out_shape=(o...  38.2 us
    unnamed x2, local copies, waits for them, and re-layouts  3.34 us

profile of v2, /device:TPU:0, one launch (start us, length us, event | category | flops | bytes accessed | tf_op | source)
XLA Modules:
  0.0 42.2 jit_solution(13172494581244451293)
XLA Ops:
  0.6 38.2 %shard_map.86 = (f32[1,256,256]{2,1,0:T(8,128)}, f32[1,256,256]{2,1,0:T(8,128)}) custom-call(bf16[1,256,8192]{2,1,0:T(8,128)(2,1)} %basis_ref.1, f32[1,8192]{1,0:T(1,128)} %sat_ref.1, f32[1,8192]{1,0:T(1,128)} %head_ref.1, f32[1,8192]{1,0:T(1,128)} %storage_ref.1, s32[16]{0:T(128)} %counts_ref.1, s32[16]{0:T(128)} %partner_ref.1, s32[16]{0:T(128)} %owner_ref.1), custom_call_target="tpu_custom_call" | custom-call | tf_op jit(solution)/shard_map/pallas_call | solution.py:373
  38.9 1.7 %copy.11 = f32[1,256,256]{2,1,0:T(8,128)} copy(f32[1,256,256]{2,1,0:T(8,128)} %get-tuple-element.4) | data formatting | bytes 524288
  40.5 1.7 %copy.12 = f32[1,256,256]{2,1,0:T(8,128)} copy(f32[1,256,256]{2,1,0:T(8,128)} %get-tuple-element.5) | data formatting | bytes 524288

commit v3 on v2

--- a/solution.py
+++ b/solution.py
@@ -68,7 +68,7 @@
     partner_ref,
     owner_ref,
     diag_ref,
-    coupling_ref,
+    face_ref,
     basis_v,
     image_v,
     coef_ref,
@@ -77,8 +77,7 @@
     face_stage,
     face_fin,
     diag_src,
-    diag_recv_0,
-    diag_recv_1,
+    diag_recv,
     diag_stage,
     diag_fin,
     inverse_ref,
@@ -86,7 +85,6 @@
     face_sems,
     diag_sems,
 ):
-    diag_recv = (diag_recv_0, diag_recv_1)
     rows_total = basis_v.shape[0]
     pieces = rows_total // piece_rows
     stride = width // pieces
@@ -160,10 +158,10 @@
     def group_rows(half, step):
         local_group = lax.rem(step + me * groups_per_piece, half_rows // ROWS)
         place = pl.multiple_of(local_group * ROWS, ROWS)
-        return place, pl.multiple_of(half * half_rows + place, ROWS)
+        return pl.multiple_of(half * half_rows + place, ROWS)
 
     def image_group(half, step):
-        place, row = group_rows(half, step)
+        row = group_rows(half, step)
         values = {}
         turned = {}
 
@@ -192,10 +190,10 @@
                 image = image - coef(3, z, j) * turn(z, j)
                 image = image - coef(4, z, j) * jnp.where(low, turn(z, j - 1), turn(z, j + 1))
                 image = image - along_z * value(1 - z, j)
-                image_v[pl.ds(place, ROWS), tile_of(z, j)] = image.astype(jnp.bfloat16)
+                image_v[pl.ds(row, ROWS), tile_of(z, j)] = image.astype(jnp.bfloat16)
 
     def face_group(half, step):
-        place, row = group_rows(half, step)
+        row = group_rows(half, step)
         keep = row + lax.broadcasted_iota(jnp.int32, (ROWS, LANES), 0) < own_count
         piece = row // piece_rows
         inner = pl.multiple_of(lax.rem(row, piece_rows), ROWS)
@@ -208,7 +206,7 @@
                     mixed = jnp.where(
                         westerly,
                         basis_v[pl.ds(row, ROWS), tile_of(z, j)].astype(jnp.float32),
-                        image_v[pl.ds(place, ROWS), tile_of(z, j)].astype(jnp.float32),
+                        image_v[pl.ds(row, ROWS), tile_of(z, j)].astype(jnp.float32),
                     )
                     if shift:
                         mixed = pltpu.roll(mixed, shift, 1)
@@ -240,14 +238,14 @@
             def _():
                 face_recv[me] = face_src[piece]
 
-    def diag_half(half):
+    def diag_whole():
         block = lax.dot_general(
             basis_v[...], image_v[...], (((1,), (1,)), ((), ())), preferred_element_type=jnp.float32
         )
         row = lax.broadcasted_iota(jnp.int32, block.shape, 0)
-        column = lax.broadcasted_iota(jnp.int32, block.shape, 1) + half * half_rows
+        column = lax.broadcasted_iota(jnp.int32, block.shape, 1)
         block = jnp.where((row < own_count) & (column < own_count), block, 0.0)
-        diag_src[half] = block.astype(jnp.bfloat16).reshape(pieces, piece_rows, half_rows)
+        diag_src[...] = block.astype(jnp.bfloat16).reshape(pieces, piece_rows, rows_total)
 
         @pl.loop(0, pieces)
         def _(step):
@@ -255,11 +253,11 @@
 
             @pl.when(piece * stride != me)
             def _():
-                first_leg(diag_src.at[half], diag_recv[half], diag_sems.at[half], piece).start()
+                first_leg(diag_src, diag_recv, diag_sems, piece).start()
 
             @pl.when(piece * stride == me)
             def _():
-                diag_recv[half][me] = diag_src[half, piece]
+                diag_recv[me] = diag_src[piece]
 
     def wait_first(src, recv, sems):
         @pl.loop(0, width)
@@ -324,25 +322,27 @@
     loads[0].wait()
     image_half(0)
     loads[1].wait()
-    diag_half(0)
     image_half(1)
-    diag_half(1)
+    diag_whole()
     face_refs = (face_src, face_recv, face_stage, face_fin, face_sems)
-    diag_refs = [
-        (diag_src.at[h], diag_recv[h], diag_stage.at[h], diag_fin.at[h], diag_sems.at[h])
-        for h in range(HALVES)
-    ]
+    diag_refs = (diag_src, diag_recv, diag_stage, diag_fin, diag_sems)
     forward(pick_face, *face_refs)
-    for h in range(HALVES):
-        forward(lambda source, h=h: diag_recv[h][source], *diag_refs[h])
-
+    forward(lambda source: diag_recv[source], *diag_refs)
     wait_second(face_stage, face_fin, face_sems)
-    both = face_fin[...].reshape(rows_total, 2 * FACE).astype(jnp.float32)
+    face_ref[...] = face_fin[...].reshape(rows_total, 2 * FACE)
+    wait_second(diag_stage, diag_fin, diag_sems)
+    diag_ref[...] = diag_fin[...].reshape(rows_total, rows_total)
+    wait_sent(*face_refs)
+    wait_sent(*diag_refs)
+
+
+def finish(diag_in, face_in, diag_ref, coupling_ref):
+    diag_ref[0] = diag_in[...].astype(jnp.float32)
     easts, wests = [], []
-    east_lane = lax.broadcasted_iota(jnp.int32, (rows_total, LANES), 1) % 4 >= 2
     for n in range(2 * FACE // LANES):
-        tile = both[:, n * LANES : (n + 1) * LANES]
-        easts.append(jnp.where(east_lane, tile, 0.0).astype(jnp.bfloat16))
+        tile = face_in[:, n * LANES : (n + 1) * LANES].astype(jnp.float32)
+        easterly = lax.broadcasted_iota(jnp.int32, tile.shape, 1) % 4 >= 2
+        easts.append(jnp.where(easterly, tile, 0.0).astype(jnp.bfloat16))
         wests.append(pltpu.roll(tile, LAT - 2, 1).astype(jnp.bfloat16))
     coupling_ref[0] = lax.dot_general(
         jnp.concatenate(easts, axis=1),
@@ -350,14 +350,6 @@
         (((1,), (1,)), ((), ())),
         preferred_element_type=jnp.float32,
     )
-    for h in range(HALVES):
-        wait_second(diag_stage.at[h], diag_fin.at[h], diag_sems.at[h])
-        diag_ref[0, :, h * half_rows : (h + 1) * half_rows] = (
-            diag_fin[h].reshape(rows_total, half_rows).astype(jnp.float32)
-        )
-    wait_sent(*face_refs)
-    for h in range(HALVES):
-        wait_sent(*diag_refs[h])
 
 
 def local(width, basis, sat_cond, head, storage, counts, partner, owner):
@@ -365,38 +357,42 @@
     cells = basis.shape[2]
     piece_rows = max(ROWS, rows // width)
     pieces = rows // piece_rows
-    half = rows // HALVES
     bf16 = jnp.bfloat16
     out = jax.ShapeDtypeStruct((1, rows, rows), jnp.float32)
     vmem = pl.BlockSpec(memory_space=pltpu.VMEM)
     smem = pl.BlockSpec(memory_space=pltpu.SMEM)
-    return pl.pallas_call(
+    diag, face = pl.pallas_call(
         functools.partial(kernel, width, piece_rows),
-        out_shape=(out, out),
+        out_shape=(
+            jax.ShapeDtypeStruct((rows, rows), bf16),
+            jax.ShapeDtypeStruct((rows, 2 * FACE), bf16),
+        ),
         in_specs=[pl.BlockSpec(memory_space=pl.ANY), vmem, vmem, vmem, smem, smem, smem],
         out_specs=(vmem, vmem),
         scratch_shapes=[
             pltpu.VMEM((rows, cells), bf16),
-            pltpu.VMEM((half, cells), bf16),
+            pltpu.VMEM((rows, cells), bf16),
             pltpu.VMEM((6, 8, cells), jnp.float32),
             pltpu.VMEM((pieces, piece_rows, 2 * FACE), bf16),
             pltpu.VMEM((width, piece_rows, 2 * FACE), bf16),
             pltpu.VMEM((width, piece_rows, 2 * FACE), bf16),
             pltpu.VMEM((pieces, piece_rows, 2 * FACE), bf16),
-            pltpu.VMEM((HALVES, pieces, piece_rows, half), bf16),
-            pltpu.VMEM((width, piece_rows, half), bf16),
-            pltpu.VMEM((width, piece_rows, half), bf16),
-            pltpu.VMEM((HALVES, width, piece_rows, half), bf16),
-            pltpu.VMEM((HALVES, pieces, piece_rows, half), bf16),
+            pltpu.VMEM((pieces, piece_rows, rows), bf16),
+            pltpu.VMEM((width, piece_rows, rows), bf16),
+            pltpu.VMEM((width, piece_rows, rows), bf16),
+            pltpu.VMEM((pieces, piece_rows, rows), bf16),
             pltpu.SMEM((width,), jnp.int32),
             pltpu.SemaphoreType.DMA((HALVES,)),
             pltpu.SemaphoreType.DMA((4, width)),
-            pltpu.SemaphoreType.DMA((HALVES, 4, width)),
+            pltpu.SemaphoreType.DMA((4, width)),
         ],
         compiler_params=pltpu.CompilerParams(
             collective_id=0, has_side_effects=True, vmem_limit_bytes=60 * 1024 * 1024
         ),
     )(basis, sat_cond, head, storage, counts, partner, owner)
+    return pl.pallas_call(
+        finish, out_shape=(out, out), in_specs=[vmem, vmem], out_specs=(vmem, vmem)
+    )(diag, face)
 
 
 def solution(mesh):

time: 42.5 us -> 38.5 us (0.906)
  local copies, waits for them, and re-layouts: 3.34 us -> 0 us
  Pallas kernels: 38.2 us -> 37.6 us
    unnamed x2 -> x0, local copies, waits for them, and re-layouts: 3.34 us -> none
    pallas_call x1 -> x2, Pallas kernels: 38.2 us -> 37.6 us  [the longest x1 35.6 us: local(): pl.pallas_call(functools.partial(kernel, width, piece_rows), out_shape=(j...]
where the time goes in v3:
time: 38.5 us; the launch traced here: 38.3 us
  Pallas kernels  37.6 us (98%)
  between operations  0.64 us (2%)
    pallas_call x1, Pallas kernels, local(): pl.pallas_call(functools.partial(kernel, width, piece_rows), out_shape=(j...  35.6 us
    pallas_call x1, Pallas kernels, local(): pl.pallas_call(finish, out_shape=(out, out), in_specs=[vmem, vmem], out_s...  2.07 us

profile of v3, /device:TPU:0, one launch (start us, length us, event | category | flops | bytes accessed | tf_op | source)
XLA Modules:
  0.0 38.3 jit_solution(10532851812388289356)
XLA Ops:
  0.6 35.6 %shard_map.86 = (bf16[256,256]{1,0:T(8,128)(2,1)}, bf16[256,512]{1,0:T(8,128)(2,1)}) custom-call(bf16[1,256,8192]{2,1,0:T(8,128)(2,1)} %basis_ref.1, f32[1,8192]{1,0:T(1,128)} %sat_ref.1, f32[1,8192]{1,0:T(1,128)} %head_ref.1, f32[1,8192]{1,0:T(1,128)} %storage_ref.1, s32[16]{0:T(128)} %counts_ref.1, s32[16]{0:T(128)} %partner_ref.1, s32[16]{0:T(128)} %owner_ref.1), custom_call_target="tpu_custom_call" | custom-call | tf_op jit(solution)/shard_map/pallas_call | solution.py:364
  36.2 2.1 %shard_map.87 = (f32[1,256,256]{2,1,0:T(8,128)}, f32[1,256,256]{2,1,0:T(8,128)}) custom-call(bf16[256,256]{1,0:T(8,128)(2,1)} %get-tuple-element.4.diag_in, bf16[256,512]{1,0:T(8,128)(2,1)} %get-tuple-element.5.face_in), custom_call_target="tpu_custom_call" | custom-call | tf_op jit(solution)/shard_map/pallas_call | solution.py:393

commit v4 on v3

--- a/solution.py
+++ b/solution.py
@@ -12,6 +12,7 @@
 FACE = 256
 LANES = 128
 ROWS = 16
+IMAGE_ROWS = 32
 TILES = LAT * LAT // LANES
 GROUP = 16
 HALVES = 2
@@ -125,7 +126,6 @@
 
     own_count = counts_ref[me]
     lane = lax.broadcasted_iota(jnp.int32, (ROWS, LANES), 1)
-    low = lane < LAT
     westerly = lane % LAT < 2
 
     def copy_to(src, dst, send_sem, recv_sem, target):
@@ -161,13 +161,14 @@
         return pl.multiple_of(half * half_rows + place, ROWS)
 
     def image_group(half, step):
-        row = group_rows(half, step)
+        row = pl.multiple_of(half * half_rows + step * IMAGE_ROWS, IMAGE_ROWS)
+        low_half = lax.broadcasted_iota(jnp.int32, (IMAGE_ROWS, LANES), 1) < LAT
         values = {}
         turned = {}
 
         def value(z, j):
             if (z, j) not in values:
-                values[z, j] = basis_v[pl.ds(row, ROWS), tile_of(z, j)].astype(jnp.float32)
+                values[z, j] = basis_v[pl.ds(row, IMAGE_ROWS), tile_of(z, j)].astype(jnp.float32)
             return values[z, j]
 
         def turn(z, j):
@@ -178,7 +179,7 @@
 
         def coef(n, z, j):
             one = coef_ref[n, :, tile_of(z, j)]
-            return jnp.concatenate([one] * (ROWS // 8), axis=0)
+            return jnp.concatenate([one] * (IMAGE_ROWS // 8), axis=0)
 
         for j in range(TILES):
             along_z = coef(5, 0, j)
@@ -188,9 +189,9 @@
                 image = image - coef(1, z, j) * pltpu.roll(own, LANES - 1, 1)
                 image = image - coef(2, z, j) * pltpu.roll(own, 1, 1)
                 image = image - coef(3, z, j) * turn(z, j)
-                image = image - coef(4, z, j) * jnp.where(low, turn(z, j - 1), turn(z, j + 1))
+                image = image - coef(4, z, j) * jnp.where(low_half, turn(z, j - 1), turn(z, j + 1))
                 image = image - along_z * value(1 - z, j)
-                image_v[pl.ds(row, ROWS), tile_of(z, j)] = image.astype(jnp.bfloat16)
+                image_v[pl.ds(row, IMAGE_ROWS), tile_of(z, j)] = image.astype(jnp.bfloat16)
 
     def face_group(half, step):
         row = group_rows(half, step)
@@ -220,7 +221,7 @@
     def image_half(half):
         piece_per_half = pieces // HALVES
 
-        @pl.loop(0, half_rows // ROWS)
+        @pl.loop(0, half_rows // IMAGE_ROWS)
         def _(step):
             image_group(half, step)
 

time: 38.5 us -> 38.2 us (level)
  no operation moved by 1% of the time
where the time goes in v4:
time: 38.2 us; the launch traced here: 38 us
  Pallas kernels  37.3 us (98%)
  between operations  0.64 us (2%)
    pallas_call x1, Pallas kernels, local(): pl.pallas_call(functools.partial(kernel, width, piece_rows), out_shape=(j...  35.3 us
    pallas_call x1, Pallas kernels, local(): pl.pallas_call(finish, out_shape=(out, out), in_specs=[vmem, vmem], out_s...  2.07 us

profile of v4, /device:TPU:0, one launch (start us, length us, event | category | flops | bytes accessed | tf_op | source)
XLA Modules:
  0.0 38.0 jit_solution(2794330451850354098)
XLA Ops:
  0.6 35.3 %shard_map.86 = (bf16[256,256]{1,0:T(8,128)(2,1)}, bf16[256,512]{1,0:T(8,128)(2,1)}) custom-call(bf16[1,256,8192]{2,1,0:T(8,128)(2,1)} %basis_ref.1, f32[1,8192]{1,0:T(1,128)} %sat_ref.1, f32[1,8192]{1,0:T(1,128)} %head_ref.1, f32[1,8192]{1,0:T(1,128)} %storage_ref.1, s32[16]{0:T(128)} %counts_ref.1, s32[16]{0:T(128)} %partner_ref.1, s32[16]{0:T(128)} %owner_ref.1), custom_call_target="tpu_custom_call" | custom-call | tf_op jit(solution)/shard_map/pallas_call | solution.py:365
  35.9 2.1 %shard_map.87 = (f32[1,256,256]{2,1,0:T(8,128)}, f32[1,256,256]{2,1,0:T(8,128)}) custom-call(bf16[256,256]{1,0:T(8,128)(2,1)} %get-tuple-element.4.diag_in, bf16[256,512]{1,0:T(8,128)(2,1)} %get-tuple-element.5.face_in), custom_call_target="tpu_custom_call" | custom-call | tf_op jit(solution)/shard_map/pallas_call | solution.py:394
